TPU v7x, 32 devices: a whole 2x2x4 slice. The times are simulated.
32 devices in a mesh: dp: 8 (over z, x), tensor: 4 (over y, core).
Axes of the slice: x: 2, y: 2, z: 4, core: 2. Of those that a mesh axis runs over, the one named last changes fastest.
Arguments:
- tokens: bfloat16 [64, 16384], P('dp', 'tensor'), may hold values from -6 to 6
- clip_act: float32 [16384], P('tensor'), may hold values from 0.5 to 4
- weight: bfloat16 [16384, 49152], P('tensor', 'dp'), may hold values from -0.046875 to 0.046875
- clip_weight: float32 [49152], P('dp'), may hold values from 0.003 to 0.03
- cotangent: bfloat16 [64, 49152], P('tensor', 'dp'), may hold values from -6 to 6
Outputs:
- projected: bfloat16 [64, 49152], P('tensor', 'dp')
- token_grad: bfloat16 [64, 16384], P('dp', 'tensor')
- weight_grad: bfloat16 [16384, 49152], P('tensor', 'dp')
- clip_act_grad: float32 [16384], P('tensor')
- clip_weight_grad: float32 [49152], P('dp')
All inputs are finite; a program needn't handle non-finite values.
Results may differ from a plain program's by a relative error of at most 0.009.
Values may be sent and summed in bfloat16 or wider, within the bound.
A program may use at most 192 MiB of HBM per device.

v0:
```python
import math

import jax
import jax.numpy as jnp
from jax import lax
from jax.sharding import PartitionSpec as P


def swapped(block, axis, bit):
    count = lax.axis_size(axis)
    route = []
    for low in range(count):
        high = low | 1 << bit
        if high != low and high < count:
            route += [(low, high), (high, low)]
    return lax.ppermute(block, axis, route)


def sylvester(order):
    index = lax.iota(jnp.int32, order)
    joined = jnp.bitwise_and(index[:, None], index[None, :])
    parity = jnp.zeros((order, order), jnp.int32)
    for bit_number in range(max(order.bit_length() - 1, 0)):
        parity = parity + jnp.bitwise_and(jnp.right_shift(joined, bit_number), 1)
    return (1 - 2 * jnp.bitwise_and(parity, 1)).astype(jnp.float32)


def local_rotate(values, norm_factor):
    row_total, width = values.shape
    levels = width.bit_length() - 1
    outer = 2 ** (levels // 2)
    inner = width // outer
    blocks = values.reshape(row_total, outer, inner)
    blocks = jnp.einsum("rab,ac->rcb", blocks, sylvester(outer), precision=lax.Precision.HIGHEST)
    blocks = jnp.einsum("rcb,bd->rcd", blocks, sylvester(inner), precision=lax.Precision.HIGHEST)
    return blocks.reshape(row_total, width) * norm_factor


def rotate(values):
    group_size = lax.axis_size("tensor")
    norm_factor = 1.0 / math.sqrt(values.shape[1] * group_size)
    mixed = local_rotate(values, norm_factor)
    position = lax.axis_index("tensor")
    for bit_number in range(group_size.bit_length() - 1):
        partner = swapped(mixed, "tensor", bit_number)
        upper = jnp.bitwise_and(jnp.right_shift(position, bit_number), 1) == 1
        mixed = jnp.where(upper, partner - mixed, mixed + partner)
    return mixed


def body(tokens, clip_act, weight, clip_weight, cotangent):
    rotated = rotate(tokens.astype(jnp.float32))
    ratio_act = rotated / clip_act
    tanh_act = jnp.tanh(ratio_act)
    quant_act = (clip_act * tanh_act).astype(jnp.bfloat16)
    slope_act = 1.0 - tanh_act * tanh_act
    edge_act = tanh_act - ratio_act * slope_act
    all_act = lax.all_gather(quant_act, "dp", axis=0, tiled=True)
    ratio_weight = weight.astype(jnp.float32) / clip_weight
    tanh_weight = jnp.tanh(ratio_weight)
    quant_weight = (clip_weight * tanh_weight).astype(jnp.bfloat16)
    block = all_act
    projected = lax.psum_scatter(
        jnp.dot(block, quant_weight, preferred_element_type=jnp.float32),
        "tensor",
        scatter_dimension=0,
        tiled=True,
    ).astype(jnp.bfloat16)
    all_cot = lax.all_gather(cotangent, "tensor", axis=0, tiled=True)
    weight_prod = lax.dot_general(
        all_act, all_cot, (((0,), (0,)), ((), ())), preferred_element_type=jnp.float32
    )
    slope_weight = 1.0 - tanh_weight * tanh_weight
    weight_grad = (weight_prod * slope_weight).astype(jnp.bfloat16)
    weight_terms = jnp.sum(weight_prod * (tanh_weight - ratio_weight * slope_weight), axis=0)
    clip_weight_grad = lax.psum(weight_terms, "tensor")
    block = all_cot
    act_prod = lax.psum_scatter(
        lax.dot_general(
            block, quant_weight, (((1,), (1,)), ((), ())), preferred_element_type=jnp.float32
        ),
        "dp",
        scatter_dimension=0,
        tiled=True,
    )
    clip_act_grad = lax.psum(jnp.sum(act_prod * edge_act, axis=0), "dp")
    pre_rotation = act_prod * slope_act
    token_grad = rotate(pre_rotation).astype(jnp.bfloat16)
    return (projected, token_grad, weight_grad, clip_act_grad, clip_weight_grad)


def solution(mesh):
    in_specs = (P("dp", "tensor"), P("tensor"), P("tensor", "dp"), P("dp"), P("tensor", "dp"))
    out_specs = (P("tensor", "dp"), P("dp", "tensor"), P("tensor", "dp"), P("tensor"), P("dp"))
    return jax.shard_map(body, mesh=mesh, in_specs=in_specs, out_specs=out_specs, check_vma=False)
```

profile of v0, /device:TPU:0, one launch (start us, length us, event | category | flops | bytes accessed | tf_op | source)
XLA Modules:
  0.0 300.6 jit_solution(2391469666778368461)
XLA Ops:
  7.2 0.0 reduce-scatter.5.cloned.1.call-start
  7.2 10.3 %all_gather.7 = bf16[64,6144]{1,0:T(8,128)(2,1)S(1)} all-gather(bf16[16,6144]{1,0:T(8,128)(2,1)} %param.9), channel_id=1, replica_groups=mesh['dp'=8,'tensor'=4] {'tensor'}, dimensions={0}, use_global_device_ids=true | all-gather | bytes 983040 | tf_op jit(solution)/shard_map/all_gather | solution.py:69
  17.5 34.4 %multiply_convert_fusion.1 = bf16[4096,6144]{1,0:T(8,128)(2,1)} fusion(f32[6144]{0:T(1024)} %param.8, bf16[4096,6144]{1,0:T(8,128)(2,1)} %param.7), kind=kLoop, calls=%fused_computation.3 | loop fusion | flops 100663296 | bytes 100687872 | tf_op jit(solution)/shard_map/convert_element_type | solution.py:61
  51.9 24.6 %convolution_bitcast_fusion = f32[64,4096]{1,0:T(8,128)} fusion(bf16[4096,6144]{1,0:T(8,128)(2,1)} %multiply_convert_fusion.1, bf16[64,6144]{1,0:T(8,128)(2,1)S(1)} %all_gather.7), kind=kOutput, calls=%fused_computation.5 | convolution fusion | flops 3221225472 | bytes 52166656 | tf_op jit(solution)/shard_map/dot_general | solution.py:79
  76.5 0.0 reduce-scatter.5.cloned.1.call-update
  76.6 0.0 reduce-scatter.3.cloned.1.call-start
  76.6 0.2 reshape.24
  76.8 0.3 convolution_bitcast_fusion.2
  77.1 0.4 convolution_multiply_fusion.1
  77.5 0.1 mul.67
  77.6 0.4 collective-permute-start
  78.1 1.0 collective-permute-done
  79.1 1.2 collective-permute-start.1
  80.2 4.7 %collective-permute-done.1 = f32[8,4096]{1,0:T(8,128)S(1)} collective-permute-done((f32[8,4096]{1,0:T(8,128)S(1)}, f32[8,4096]{1,0:T(8,128)S(1)}, u32[]{:S(2)}, u32[]{:S(2)}) %collective-permute-start.1) | collective-permute-done | bytes 131104 | tf_op jit(solution)/shard_map/ppermute | solution.py:16
  84.9 56.5 %reduce-scatter.5.cloned.1.call-done = f32[8,4096]{1,0:T(8,128)} async-done(((f32[64,4096]{1,0:T(8,128)}), f32[8,4096]{1,0:T(8,128)}) %reduce-scatter.5.cloned.1.call-update) | async-done | bytes 131088 | tf_op jit(solution)/shard_map/reduce_scatter | solution.py:78
  141.4 1.6 multiply_reduce_fusion.1
  143.0 0.9 fusion
  144.0 0.1 reshape.25
  144.1 0.4 convolution_bitcast_fusion.1
  144.5 0.4 convolution_multiply_fusion
  144.9 0.1 mul.74
  145.0 0.1 collective-permute-start.2
  145.1 31.7 %all_gather.6 = bf16[64,4096]{1,0:T(8,128)(2,1)S(1)} all-gather(bf16[8,4096]{1,0:T(8,128)(2,1)S(1)} %get-tuple-element.10), channel_id=1, replica_groups=mesh['dp'=8,'tensor'=4] {'dp'}, dimensions={0}, use_global_device_ids=true | all-gather | bytes 589824 | tf_op jit(solution)/shard_map/all_gather | solution.py:58
  176.8 20.9 %fusion.33 = f32[64,6144]{1,0:T(8,128)} fusion(bf16[64,4096]{1,0:T(8,128)(2,1)S(1)} %all_gather.6, bf16[4096,6144]{1,0:T(8,128)(2,1)} %multiply_convert_fusion.1), kind=kOutput, calls=%fused_computation.51 | convolution fusion | flops 3221225472 | bytes 52428800 | tf_op jit(solution)/shard_map/dot_general | solution.py:64
  197.7 0.0 reduce-scatter.3.cloned.1.call-update
  197.7 0.7 add_select_fusion
  198.4 1.4 collective-permute-start.3
  199.9 44.1 %multiply_reduce_fusion = (f32[6144]{0:T(1024)S(1)}, bf16[4096,6144]{1,0:T(8,128)(2,1)}) fusion(f32[6144]{0:T(1024)S(1)} %copy-done.3, bf16[4096,6144]{1,0:T(8,128)(2,1)} %param.7, bf16[64,4096]{1,0:T(8,128)(2,1)S(1)} %all_gather.6, bf16[64,6144]{1,0:T(8,128)(2,1)S(1)} %all_gather.7), kind=kOutput, calls=%fused_computation | convolution fusion | flops 3472877568 | bytes 102023168 | tf_op jit(solution)/shard_map/dot_general | solution.py:70
  243.9 35.6 %psum.14 = f32[4096]{0:T(1024)} all-reduce(f32[4096]{0:T(1024)S(1)} %copy-done.1), channel_id=1, replica_groups=mesh['dp'=8,'tensor'=4] {'dp'}, use_global_device_ids=true, to_apply=%region_3.4 | all-reduce | flops 4096 | bytes 32768 | tf_op jit(solution)/shard_map/psum | solution.py:86
  279.5 10.9 %psum.15 = f32[6144]{0:T(1024)} all-reduce(f32[6144]{0:T(1024)S(1)} %get-tuple-element.7), channel_id=1, replica_groups=mesh['dp'=8,'tensor'=4] {'tensor'}, use_global_device_ids=true, to_apply=%region_5.6 | all-reduce | flops 6144 | bytes 49152 | tf_op jit(solution)/shard_map/psum | solution.py:76
  290.4 1.6 select_convert_fusion
  292.0 1.7 convert_element_type.35
  (12 shorter events, 0.0 us)
Async XLA Ops:
  7.2 134.2 %reduce-scatter.5.cloned.1.call-start = ((), (), s32[]{:S(2)}) async-start(), calls=%async_computation.3 | async-start | bytes 1179648 | tf_op jit(solution)/shard_map/reduce_scatter | solution.py:78
  51.9 24.7 %copy-start = (bf16[8,4096]{1,0:T(8,128)(2,1)S(1)}, bf16[8,4096]{1,0:T(8,128)(2,1)}, u32[]{:S(2)}) copy-start(bf16[8,4096]{1,0:T(8,128)(2,1)} %param.5) | copy-start | bytes 196612
  51.9 89.5 %copy-start.2 = (f32[4096]{0:T(1024)S(1)}, f32[4096]{0:T(1024)}, u32[]{:S(2)}) copy-start(f32[4096]{0:T(1024)} %param.6) | copy-start | bytes 49156
  76.5 123.3 %copy-start.3 = (f32[6144]{0:T(1024)S(1)}, f32[6144]{0:T(1024)}, u32[]{:S(2)}) copy-start(f32[6144]{0:T(1024)} %param.8) | copy-start | bytes 73732
  76.6 215.5 %reduce-scatter.3.cloned.1.call-start = ((), (), s32[]{:S(2)}) async-start(), calls=%async_computation.2 | async-start | bytes 1966080 | tf_op jit(solution)/shard_map/reduce_scatter | solution.py:63
  77.6 1.4 collective-permute-start
  79.1 5.8 %collective-permute-start.1 = (f32[8,4096]{1,0:T(8,128)S(1)}, f32[8,4096]{1,0:T(8,128)S(1)}, u32[]{:S(2)}, u32[]{:S(2)}) collective-permute-start(f32[8,4096]{1,0:T(8,128)S(1)} %add_select_fusion.1), channel_id=1, source_target_pairs={{0,2},{2,0},{1,3},{3,1},{4,6},{6,4},{5,7},{7,5},{8,10},{10,8},{9,1... | collective-permute-start | bytes 393224 | tf_op jit(solution)/shard_map/ppermute | solution.py:16
  145.0 52.7 %collective-permute-start.2 = (f32[8,4096]{1,0:T(8,128)S(1)}, f32[8,4096]{1,0:T(8,128)S(1)}, u32[]{:S(2)}, u32[]{:S(2)}) collective-permute-start(f32[8,4096]{1,0:T(8,128)S(1)} %mul.74), channel_id=1, source_target_pairs={{0,1},{1,0},{2,3},{3,2},{4,5},{5,4},{6,7},{7,6},{8,9},{9,8},{10,11... | collective-permute-start | bytes 393224 | tf_op jit(solution)/shard_map/ppermute | solution.py:16
  198.4 92.0 %collective-permute-start.3 = (f32[8,4096]{1,0:T(8,128)}, f32[8,4096]{1,0:T(8,128)}, u32[]{:S(2)}, u32[]{:S(2)}) collective-permute-start(f32[8,4096]{1,0:T(8,128)} %add_select_fusion), channel_id=1, source_target_pairs={{0,2},{2,0},{1,3},{3,1},{4,6},{6,4},{5,7},{7,5},{8,10},{10,8},{9,1... | collective-permute-start | bytes 393224 | tf_op jit(solution)/shard_map/ppermute | solution.py:16
  199.8 44.1 %copy-start.1 = (f32[4096]{0:T(1024)S(1)}, f32[4096]{0:T(1024)}, u32[]{:S(2)}) copy-start(f32[4096]{0:T(1024)} %get-tuple-element.5) | copy-start | bytes 49156
Sparse Core Ops, SparseCore 0:
  76.7 64.6 reduce-scatter.4
  197.8 27.1 reduce-scatter.2
where the time goes:
time: 301 us
  matrix products  91.1 us (30%)
  blocking collectives  88.5 us (29%)
  waiting for transfers between devices  62.2 us (21%)
  other arithmetic  40.9 us (14%)
  between operations  14.1 us (5%)
  starting transfers between devices  3.16 us (1%)
    reduce_scatter x1, waiting for transfers between devices, body(): lax.psum_scatter(lax.dot_general(block, quant_weight, (((1,), (1,)), ((),...  56.5 us
    dot_general x1, matrix products, body(): lax.dot_general(all_act, all_cot, (((0,), (0,)), ((), ())), preferred_ele...  44.1 us
    psum x1, blocking collectives, body(): clip_act_grad = lax.psum(jnp.sum(act_prod * edge_act, axis=0), 'dp')  35.6 us
    convert_element_type x1, other arithmetic, body(): quant_weight = (clip_weight * tanh_weight).astype(jnp.bfloat16)  34.4 us
    all_gather x1, blocking collectives, body(): all_act = lax.all_gather(quant_act, 'dp', axis=0, tiled=True)  31.7 us
    dot_general x1, matrix products, body(): lax.dot_general(block, quant_weight, (((1,), (1,)), ((), ())), preferred_...  24.6 us
    dot_general x1, matrix products, body(): jnp.dot(block, quant_weight, preferred_element_type=jnp.float32)  20.9 us
    psum x1, blocking collectives, body(): clip_weight_grad = lax.psum(weight_terms, 'tensor')  10.9 us
  transfers between devices with their start and end apart: 6, of which 3 were waited for; matrix products, arithmetic and copies ran while one was open for 23% of the time, Pallas kernels for 0%

commit v1 on v0

v1 whole, which is shorter than its diff:
```python
import functools
import math

import jax
import jax.numpy as jnp
import numpy as np
from jax import lax
from jax.experimental import pallas as pl
from jax.experimental.pallas import tpu as pltpu
from jax.sharding import PartitionSpec as P

MESH = pl.DeviceIdType.MESH
F32, BF16 = jnp.float32, jnp.bfloat16
LANES = 128


def hadamard_tile():
    index = np.arange(LANES)
    joined = index[:, None] & index[None, :]
    parity = np.zeros_like(joined)
    for bit in range(7):
        parity ^= (joined >> bit) & 1
    return (1 - 2 * parity).astype(np.float32)


def sign_of(a, b, count):
    total = 0
    for bit in range(count.bit_length() - 1):
        total = total + ((a // 2**bit) % 2) * ((b // 2**bit) % 2)
    return (1 - 2 * (total % 2)).astype(F32)


def local_rotate(values, had):
    rows, width = values.shape
    count = width // LANES
    blocks = [values[:, i * LANES : (i + 1) * LANES] for i in range(count)]
    step = 1
    while step < count:
        mixed = list(blocks)
        for i in range(count):
            if i & step == 0:
                mixed[i] = blocks[i] + blocks[i + step]
                mixed[i + step] = blocks[i] - blocks[i + step]
        blocks = mixed
        step *= 2
    stacked = jnp.concatenate(blocks, axis=0)
    out = jnp.dot(stacked, had, preferred_element_type=F32, precision=lax.Precision.HIGHEST)
    return jnp.concatenate([out[i * rows : (i + 1) * rows] for i in range(count)], axis=1)


def fold(values):
    half = values.shape[1] // 2
    return jnp.concatenate([values[:, :half], values[:, half:]], axis=0)


def unfold(values):
    half = values.shape[0] // 2
    return jnp.concatenate([values[:half], values[half:]], axis=1)


def greet(tn, dn, me_t, me_d):
    barrier = pltpu.get_barrier_semaphore()
    for k in range(1, tn):
        pl.semaphore_signal(
            barrier, inc=1, device_id=(me_d, (me_t + k) % tn), device_id_type=MESH
        )
    for k in range(1, dn):
        pl.semaphore_signal(
            barrier, inc=1, device_id=((me_d + k) % dn, me_t), device_id_type=MESH
        )
    pl.semaphore_wait(barrier, tn + dn - 2)


def start_copy(src, dst, sems, k, device):
    copy = pltpu.make_async_remote_copy(
        src_ref=src,
        dst_ref=dst,
        send_sem=sems.at[0, k],
        recv_sem=sems.at[1, k],
        device_id=device,
        device_id_type=MESH,
    )
    copy.start()
    return copy


def gather_kernel(
    tn, dn, norm,
    tok_ref, clip_ref, cot_ref, had_ref,
    allcot_ref, allact_ref, slope_ref, edge_ref,
    tok_send, tok_buf, act_send, act_buf, cot_buf,
    tok_sems, cot_sems, act_sems,
):
    me_d, me_t = lax.axis_index("dp"), lax.axis_index("tensor")
    mine = tok_ref[...].astype(F32)
    tok_send[...] = fold(mine).astype(BF16)
    greet(tn, dn, me_t, me_d)
    tok_copies, cot_copies, act_copies = [], [], []
    for k in range(1, tn):
        device = (me_d, (me_t + k) % tn)
        tok_copies.append(start_copy(tok_send, tok_buf.at[k - 1], tok_sems, k - 1, device))
    for k in range(1, tn):
        device = (me_d, (me_t + k) % tn)
        cot_copies.append(start_copy(cot_ref, cot_buf.at[me_t], cot_sems, k - 1, device))
    cot_buf[me_t] = cot_ref[...]
    mixed = mine * sign_of(me_t, me_t, tn)
    for k in range(1, tn):
        tok_copies[k - 1].wait()
        sender = (me_t + tn - k) % tn
        mixed = mixed + unfold(tok_buf[k - 1].astype(F32)) * sign_of(me_t, sender, tn)
    rotated = local_rotate(mixed, had_ref[...]) * norm
    clip = clip_ref[...]
    ratio = rotated / clip
    act = jnp.tanh(ratio)
    act_send[...] = fold(clip * act).astype(BF16)
    for k in range(1, dn):
        device = ((me_d + k) % dn, me_t)
        act_copies.append(start_copy(act_send, act_buf.at[me_d], act_sems, k - 1, device))
    act_buf[me_d] = act_send[...]
    slope = 1.0 - act * act
    slope_ref[...] = slope
    edge_ref[...] = act - ratio * slope
    for copy in cot_copies:
        copy.wait()
    group = cot_ref.shape[0]
    for j in range(tn):
        allcot_ref[j * group : (j + 1) * group, :] = cot_buf[j]
    for copy in act_copies:
        copy.wait()
    rows = tok_ref.shape[0]
    for j in range(0, dn, 2):
        pair = [unfold(act_buf[j + i].astype(F32)) for i in range(2)]
        allact_ref[j * rows : (j + 2) * rows, :] = jnp.concatenate(pair, axis=0).astype(BF16)


def weight_kernel(chunk, act_ref, cot_ref, clip_ref, inv_ref, w_ref, grad_ref, actp_ref, proj_ref, csum_ref):
    first = pl.program_id(0) == 0
    depth, width = w_ref.shape

    @pl.when(first)
    def _():
        proj_ref[...] = jnp.zeros_like(proj_ref)
        csum_ref[...] = jnp.zeros_like(csum_ref)

    actp_ref[...] = jnp.zeros_like(actp_ref)
    act = act_ref[...]
    act_t = act.astype(F32).T.astype(BF16)

    def one(c, carry):
        cols = pl.ds(pl.multiple_of(c * chunk, chunk), chunk)
        cot = cot_ref[:, cols]
        prod = jnp.dot(act_t, cot, preferred_element_type=F32)
        ratio = w_ref[:, cols].astype(F32) * inv_ref[:, cols]
        tanh = jnp.tanh(ratio)
        quant = (clip_ref[:, cols] * tanh).astype(BF16)
        proj_ref[:, cols] += jnp.dot(act, quant, preferred_element_type=F32)
        actp_ref[...] += lax.dot_general(
            cot, quant, (((1,), (1,)), ((), ())), preferred_element_type=F32
        )
        grad = prod * (1.0 - tanh * tanh)
        grad_ref[:, cols] = grad.astype(BF16)
        terms = prod * tanh - ratio * grad
        csum_ref[:, cols] += jnp.sum(terms.reshape(depth // 8, 8, chunk), axis=0)
        return carry

    lax.fori_loop(0, width // chunk, one, 0)


def reduce_kernel(
    tn, dn, norm,
    actp_ref, proj_ref, csum_ref, slope_ref, edge_ref, had_ref,
    out_ref, tokg_ref, cag_ref, cwg_ref,
    act_send, act_buf, proj_send, proj_buf, cs_send, cs_buf, rot_send, rot_buf, ca_send, ca_buf,
    act_sems, proj_sems, cs_sems, rot_sems, ca_sems,
):
    me_d, me_t = lax.axis_index("dp"), lax.axis_index("tensor")
    rows = slope_ref.shape[0]
    group = out_ref.shape[0]
    for j in range(dn):
        act_send[j] = fold(actp_ref[j * rows : (j + 1) * rows, :]).astype(BF16)
    greet(tn, dn, me_t, me_d)
    act_copies, proj_copies, cs_copies, rot_copies, ca_copies = [], [], [], [], []
    for k in range(1, dn):
        peer = (me_d + k) % dn
        act_copies.append(
            start_copy(act_send.at[peer], act_buf.at[k - 1], act_sems, k - 1, (peer, me_t))
        )
    for j in range(tn):
        proj_send[j] = proj_ref[j * group : (j + 1) * group, :].astype(BF16)
    for k in range(1, tn):
        peer = (me_t + k) % tn
        proj_copies.append(
            start_copy(proj_send.at[peer], proj_buf.at[k - 1], proj_sems, k - 1, (me_d, peer))
        )
    cs_send[...] = jnp.sum(csum_ref[...], axis=0, keepdims=True)
    cs_buf[me_t] = cs_send[...]
    for k in range(1, tn):
        peer = (me_t + k) % tn
        cs_copies.append(start_copy(cs_send, cs_buf.at[me_t], cs_sems, k - 1, (me_d, peer)))
    total = actp_ref[pl.ds(pl.multiple_of(me_d * rows, rows), rows), :]
    for k in range(1, dn):
        act_copies[k - 1].wait()
        total = total + unfold(act_buf[k - 1].astype(F32))
    ca_send[...] = jnp.sum(total * edge_ref[...], axis=0, keepdims=True)
    mixed = local_rotate(total * slope_ref[...], had_ref[...]) * norm
    rot_send[...] = fold(mixed).astype(BF16)
    for k in range(1, tn):
        peer = (me_t + k) % tn
        rot_copies.append(start_copy(rot_send, rot_buf.at[k - 1], rot_sems, k - 1, (me_d, peer)))
    for k in range(1, dn):
        peer = (me_d + k) % dn
        ca_copies.append(start_copy(ca_send, ca_buf.at[me_d], ca_sems, k - 1, (peer, me_t)))
    ca_buf[me_d] = ca_send[...]
    own = proj_ref[pl.ds(pl.multiple_of(me_t * group, group), group), :]
    for k in range(1, tn):
        proj_copies[k - 1].wait()
        own = own + proj_buf[k - 1].astype(F32)
    out_ref[...] = own.astype(BF16)
    for copy in cs_copies:
        copy.wait()
    weight_sum = cs_buf[0]
    for j in range(1, tn):
        weight_sum = weight_sum + cs_buf[j]
    cwg_ref[...] = weight_sum
    result = mixed * sign_of(me_t, me_t, tn)
    for k in range(1, tn):
        rot_copies[k - 1].wait()
        sender = (me_t + tn - k) % tn
        result = result + unfold(rot_buf[k - 1].astype(F32)) * sign_of(me_t, sender, tn)
    tokg_ref[...] = result.astype(BF16)
    for copy in ca_copies:
        copy.wait()
    act_sum = ca_buf[0]
    for j in range(1, dn):
        act_sum = act_sum + ca_buf[j]
    cag_ref[...] = act_sum


def body(tn, dn, tokens, clip_act, weight, clip_weight, cotangent):
    rows, width = tokens.shape
    group, hidden = cotangent.shape
    all_rows = rows * dn
    norm = 1.0 / math.sqrt(width * tn)
    had = jnp.asarray(hadamard_tile())
    vmem = pl.BlockSpec(memory_space=pltpu.VMEM)
    sems = lambda n: pltpu.SemaphoreType.DMA((2, n))
    folded = (2 * rows, width // 2)
    all_cot, all_act, slope_act, edge_act = pl.pallas_call(
        functools.partial(gather_kernel, tn, dn, norm),
        out_shape=(
            jax.ShapeDtypeStruct((all_rows, hidden), BF16),
            jax.ShapeDtypeStruct((all_rows, width), BF16),
            jax.ShapeDtypeStruct((rows, width), F32),
            jax.ShapeDtypeStruct((rows, width), F32),
        ),
        in_specs=[vmem] * 4,
        out_specs=(vmem,) * 4,
        scratch_shapes=[
            pltpu.VMEM(folded, BF16),
            pltpu.VMEM((tn - 1,) + folded, BF16),
            pltpu.VMEM(folded, BF16),
            pltpu.VMEM((dn,) + folded, BF16),
            pltpu.VMEM((tn, group, hidden), BF16),
            sems(tn - 1), sems(tn - 1), sems(dn - 1),
        ],
        compiler_params=pltpu.CompilerParams(
            collective_id=0, has_side_effects=True, vmem_limit_bytes=48 * 2**20
        ),
        name="gather",
    )(tokens, clip_act.reshape(1, -1), cotangent, had)

    depth = 256
    chunk = next(c for c in (1024, 768, 512, 256, 128) if hidden % c == 0)
    clip_row = clip_weight.reshape(1, -1)
    grad, act_prod, proj, clip_sum = pl.pallas_call(
        functools.partial(weight_kernel, chunk),
        grid=(width // depth,),
        out_shape=(
            jax.ShapeDtypeStruct((width, hidden), BF16),
            jax.ShapeDtypeStruct((all_rows, width), F32),
            jax.ShapeDtypeStruct((all_rows, hidden), F32),
            jax.ShapeDtypeStruct((8, hidden), F32),
        ),
        in_specs=[
            pl.BlockSpec((all_rows, depth), lambda i: (0, i)),
            pl.BlockSpec((all_rows, hidden), lambda i: (0, 0)),
            pl.BlockSpec((1, hidden), lambda i: (0, 0)),
            pl.BlockSpec((1, hidden), lambda i: (0, 0)),
            pl.BlockSpec((depth, hidden), lambda i: (i, 0)),
        ],
        out_specs=(
            pl.BlockSpec((depth, hidden), lambda i: (i, 0)),
            pl.BlockSpec((all_rows, depth), lambda i: (0, i)),
            pl.BlockSpec((all_rows, hidden), lambda i: (0, 0)),
            pl.BlockSpec((8, hidden), lambda i: (0, 0)),
        ),
        compiler_params=pltpu.CompilerParams(vmem_limit_bytes=48 * 2**20),
        name="weights",
    )(all_act, all_cot, clip_row, 1.0 / clip_row, weight)

    projected, token_grad, clip_act_grad, clip_weight_grad = pl.pallas_call(
        functools.partial(reduce_kernel, tn, dn, norm),
        out_shape=(
            jax.ShapeDtypeStruct((group, hidden), BF16),
            jax.ShapeDtypeStruct((rows, width), BF16),
            jax.ShapeDtypeStruct((1, width), F32),
            jax.ShapeDtypeStruct((1, hidden), F32),
        ),
        in_specs=[vmem] * 6,
        out_specs=(vmem,) * 4,
        scratch_shapes=[
            pltpu.VMEM((dn,) + folded, BF16),
            pltpu.VMEM((dn - 1,) + folded, BF16),
            pltpu.VMEM((tn, group, hidden), BF16),
            pltpu.VMEM((tn - 1, group, hidden), BF16),
            pltpu.VMEM((1, hidden), F32),
            pltpu.VMEM((tn, 1, hidden), F32),
            pltpu.VMEM(folded, BF16),
            pltpu.VMEM((tn - 1,) + folded, BF16),
            pltpu.VMEM((1, width), F32),
            pltpu.VMEM((dn, 1, width), F32),
            sems(dn - 1), sems(tn - 1), sems(tn - 1), sems(tn - 1), sems(dn - 1),
        ],
        compiler_params=pltpu.CompilerParams(
            collective_id=1, has_side_effects=True, vmem_limit_bytes=48 * 2**20
        ),
        name="reduce",
    )(act_prod, proj, clip_sum, slope_act, edge_act, had)
    return projected, token_grad, grad, clip_act_grad.reshape(-1), clip_weight_grad.reshape(-1)


def solution(mesh):
    in_specs = (P("dp", "tensor"), P("tensor"), P("tensor", "dp"), P("dp"), P("tensor", "dp"))
    out_specs = (P("tensor", "dp"), P("dp", "tensor"), P("tensor", "dp"), P("tensor"), P("dp"))
    local = functools.partial(body, mesh.shape["tensor"], mesh.shape["dp"])
    return jax.shard_map(local, mesh=mesh, in_specs=in_specs, out_specs=out_specs, check_vma=False)
```

time: 301 us -> 122 us (0.41)
  Pallas kernels: 0 us -> 114 us
  matrix products: 91.1 us -> 0 us
  blocking collectives: 88.5 us -> 0 us
  waiting for transfers between devices: 62.2 us -> 0 us
  other arithmetic: 40.9 us -> 0.75 us
  between operations: 14.1 us -> 0.67 us
  local copies, waits for them, and re-layouts: 0.53 us -> 6.58 us
  starting transfers between devices: 3.16 us -> 0 us
    pallas_call x0 -> x3, Pallas kernels: none -> 114 us  [the longest x1 66.7 us: body(): pl.pallas_call(functools.partial(weight_kernel, chunk), grid=(width // de...]
    dot_general x7 -> x0, matrix products: 91.1 us -> none  [the longest x1 44.1 us: body(): lax.dot_general(all_act, all_cot, (((0,), (0,)), ((), ())), preferred_ele...]
    reduce_scatter x2 -> x0, waiting for transfers between devices: 56.5 us -> none  [the longest x1 56.5 us: body(): lax.psum_scatter(lax.dot_general(block, quant_weight, (((1,), (1,)), ((),...]
    psum x2 -> x0, blocking collectives: 46.5 us -> none  [the longest x1 35.6 us: body(): clip_act_grad = lax.psum(jnp.sum(act_prod * edge_act, axis=0), 'dp')]
    all_gather x2 -> x0, blocking collectives: 42 us -> none  [the longest x1 31.7 us: body(): all_act = lax.all_gather(quant_act, 'dp', axis=0, tiled=True)]
    convert_element_type x3 -> x0, other arithmetic: 37.7 us -> none  [the longest x1 34.4 us: body(): quant_weight = (clip_weight * tanh_weight).astype(jnp.bfloat16)]
    unnamed x8 -> x16, local copies, waits for them, and re-layouts: 0.02 us -> 6.58 us
    ppermute x4 -> x0, waiting for transfers between devices: 5.65 us -> none  [swapped(): return lax.ppermute(block, axis, route)]
  transfers between devices with their start and end apart: 6 -> 0, of which waited for: 3 -> 0; matrix products, arithmetic and copies ran while one was open for 23% -> 0% of each run, Pallas kernels for 0% -> 0%
where the time goes in v1:
time: 122 us
  Pallas kernels  114 us (93%)
  local copies, waits for them, and re-layouts  6.58 us (5%)
    pallas_call x1, Pallas kernels, body(): pl.pallas_call(functools.partial(weight_kernel, chunk), grid=(width // de...  66.7 us
    pallas_call x1, Pallas kernels, body(): pl.pallas_call(functools.partial(reduce_kernel, tn, dn, norm), out_shape=...  27.2 us
    pallas_call x1, Pallas kernels, body(): pl.pallas_call(functools.partial(gather_kernel, tn, dn, norm), out_shape=...  20.2 us
    unnamed x16, local copies, waits for them, and re-layouts  6.58 us

profile of v1, /device:TPU:0, one launch (start us, length us, event | category | flops | bytes accessed | tf_op | source)
XLA Modules:
  0.0 122.0 jit_solution(1513859602311811066)
XLA Ops:
  0.6 0.7 broadcast_divide_fusion
  1.4 0.0 copy-start
  1.4 0.8 copy-done
  2.2 0.0 copy-start.2
  2.2 0.9 copy-done.2
  3.1 0.0 copy-start.4
  3.1 0.8 copy-done.4
  4.0 0.0 copy-start.5
  4.0 0.7 copy-done.5
  4.7 0.0 copy-start.1
  4.7 20.2 %gather.1 = (bf16[64,6144]{1,0:T(8,128)(2,1)S(1)}, bf16[64,4096]{1,0:T(8,128)(2,1)S(1)}, f32[8,4096]{1,0:T(8,128)S(1)}, f32[8,4096]{1,0:T(8,128)S(1)}) custom-call(bf16[8,4096]{1,0:T(8,128)(2,1)S(1)} %copy-done.4, f32[1,4096]{1,0:T(1,128)S(1)} %bitcast.9, bf16[16,6144]{1,0:T(8,128)(2,1)S(1)} %copy-done.2, f32[128,128]{1,0:T(8,128)S(1)} %copy-done), custom_call_target="tpu_custom_call" | custom-call | tf_op jit(solution)/shard_map/gather/pallas_call | solution.py:248
  24.9 0.0 copy-start.3
  24.9 0.7 copy-done.3
  25.7 66.7 %weights.1 = (bf16[4096,6144]{1,0:T(8,128)(2,1)}, f32[64,4096]{1,0:T(8,128)S(1)}, f32[64,6144]{1,0:T(8,128)S(1)}, f32[8,6144]{1,0:T(8,128)S(1)}) custom-call(bf16[64,4096]{1,0:T(8,128)(2,1)S(1)} %get-tuple-element.17.act_ref, bf16[64,6144]{1,0:T(8,128)(2,1)S(1)} %get-tuple-element.18.cot_ref, f32[1,6144]{1,0:T(1,128)S(1)} %bitcast.5, f32[1,6144]{1,0:T(1,128)S(1)} %bitcast.6, ...), custom_call_target="tpu_custom_call" | custom-call | tf_op jit(solution)/shard_map/weights/pallas_call | solution.py:275
  92.3 0.0 copy-done.1
  92.3 27.2 %reduce.1 = (bf16[16,6144]{1,0:T(8,128)(2,1)S(1)}, bf16[8,4096]{1,0:T(8,128)(2,1)S(1)}, f32[1,4096]{1,0:T(1,128)S(1)}, f32[1,6144]{1,0:T(1,128)S(1)}) custom-call(f32[64,4096]{1,0:T(8,128)S(1)} %get-tuple-element.19.actp_ref, f32[64,6144]{1,0:T(8,128)S(1)} %get-tuple-element.20.proj_ref, f32[8,6144]{1,0:T(8,128)S(1)} %get-tuple-element.21.csum_ref, ...), custom_call_target="tpu_custom_call" | custom-call | tf_op jit(solution)/shard_map/reduce/pallas_call | solution.py:301
  119.5 0.7 copy.15
  120.2 0.6 copy.16
  120.8 0.6 copy.17
  121.4 0.6 copy.18
Async XLA Ops:
  1.4 0.8 copy-start
  2.2 0.9 copy-start.2
  3.1 0.8 copy-start.4
  4.0 0.7 copy-start.5
  4.7 87.6 %copy-start.1 = (f32[128,128]{1,0:T(8,128)S(1)}, f32[128,128]{1,0:T(8,128)}, u32[]{:S(2)}) copy-start(f32[128,128]{1,0:T(8,128)} %constant.4.clone.had_ref) | copy-start | bytes 196612
  24.9 0.7 copy-start.3

commit v2 on v1

--- a/solution.py
+++ b/solution.py
@@ -88,28 +88,44 @@
     tn, dn, norm,
     tok_ref, clip_ref, cot_ref, had_ref,
     allcot_ref, allact_ref, slope_ref, edge_ref,
-    tok_send, tok_buf, act_send, act_buf, cot_buf,
-    tok_sems, cot_sems, act_sems,
+    tok_send, tok_buf, act_send, act_buf, cot_buf, tok_own, clip_own, had_own,
+    tok_sems, cot_sems, act_sems, own_sems,
 ):
     me_d, me_t = lax.axis_index("dp"), lax.axis_index("tensor")
-    mine = tok_ref[...].astype(F32)
+    loads = [
+        pltpu.make_async_copy(src, dst, own_sems.at[i])
+        for i, (src, dst) in enumerate(
+            [
+                (tok_ref, tok_own),
+                (cot_ref, cot_buf.at[me_t]),
+                (clip_ref, clip_own),
+                (had_ref, had_own),
+            ]
+        )
+    ]
+    for load in loads:
+        load.start()
+    loads[0].wait()
+    mine = tok_own[...].astype(F32)
     tok_send[...] = fold(mine).astype(BF16)
     greet(tn, dn, me_t, me_d)
     tok_copies, cot_copies, act_copies = [], [], []
     for k in range(1, tn):
         device = (me_d, (me_t + k) % tn)
         tok_copies.append(start_copy(tok_send, tok_buf.at[k - 1], tok_sems, k - 1, device))
+    loads[1].wait()
     for k in range(1, tn):
         device = (me_d, (me_t + k) % tn)
-        cot_copies.append(start_copy(cot_ref, cot_buf.at[me_t], cot_sems, k - 1, device))
-    cot_buf[me_t] = cot_ref[...]
+        cot_copies.append(start_copy(cot_buf.at[me_t], cot_buf.at[me_t], cot_sems, k - 1, device))
+    loads[2].wait()
+    loads[3].wait()
     mixed = mine * sign_of(me_t, me_t, tn)
     for k in range(1, tn):
         tok_copies[k - 1].wait()
         sender = (me_t + tn - k) % tn
         mixed = mixed + unfold(tok_buf[k - 1].astype(F32)) * sign_of(me_t, sender, tn)
-    rotated = local_rotate(mixed, had_ref[...]) * norm
-    clip = clip_ref[...]
+    rotated = local_rotate(mixed, had_own[...]) * norm
+    clip = clip_own[...]
     ratio = rotated / clip
     act = jnp.tanh(ratio)
     act_send[...] = fold(clip * act).astype(BF16)
@@ -133,37 +149,51 @@
         allact_ref[j * rows : (j + 2) * rows, :] = jnp.concatenate(pair, axis=0).astype(BF16)
 
 
-def weight_kernel(chunk, act_ref, cot_ref, clip_ref, inv_ref, w_ref, grad_ref, actp_ref, proj_ref, csum_ref):
-    first = pl.program_id(0) == 0
+def weight_kernel(
+    chunk, piece,
+    act_ref, cot_ref, clip_ref, w_ref, grad_ref, actp_ref, proj_ref, csum_ref, quant_ref, inv_ref,
+):
     depth, width = w_ref.shape
 
-    @pl.when(first)
+    @pl.when(pl.program_id(0) == 0)
     def _():
         proj_ref[...] = jnp.zeros_like(proj_ref)
         csum_ref[...] = jnp.zeros_like(csum_ref)
+        inv_ref[...] = 1.0 / clip_ref[...]
 
     actp_ref[...] = jnp.zeros_like(actp_ref)
     act = act_ref[...]
     act_t = act.astype(F32).T.astype(BF16)
 
-    def one(c, carry):
-        cols = pl.ds(pl.multiple_of(c * chunk, chunk), chunk)
-        cot = cot_ref[:, cols]
-        prod = jnp.dot(act_t, cot, preferred_element_type=F32)
-        ratio = w_ref[:, cols].astype(F32) * inv_ref[:, cols]
-        tanh = jnp.tanh(ratio)
-        quant = (clip_ref[:, cols] * tanh).astype(BF16)
+    def products(start):
+        cols = slice(start, start + chunk)
+        quant = quant_ref[:, cols]
         proj_ref[:, cols] += jnp.dot(act, quant, preferred_element_type=F32)
         actp_ref[...] += lax.dot_general(
-            cot, quant, (((1,), (1,)), ((), ())), preferred_element_type=F32
-        )
-        grad = prod * (1.0 - tanh * tanh)
-        grad_ref[:, cols] = grad.astype(BF16)
-        terms = prod * tanh - ratio * grad
-        csum_ref[:, cols] += jnp.sum(terms.reshape(depth // 8, 8, chunk), axis=0)
-        return carry
-
-    lax.fori_loop(0, width // chunk, one, 0)
+            cot_ref[:, cols], quant, (((1,), (1,)), ((), ())), preferred_element_type=F32
+        )
+
+    for start in range(0, width, chunk):
+        for sub in range(start, start + chunk, 256):
+            cols = slice(sub, sub + 256)
+            prod_all = jnp.dot(act_t, cot_ref[:, cols], preferred_element_type=F32)
+            inv = inv_ref[:, cols]
+            clip = clip_ref[:, cols]
+            total = csum_ref[:, cols]
+            for row in range(0, depth, piece):
+                rows = slice(row, row + piece)
+                prod = prod_all[rows]
+                ratio = w_ref[rows, cols].astype(F32) * inv
+                tanh = jnp.tanh(ratio)
+                quant_ref[rows, cols] = (clip * tanh).astype(BF16)
+                grad = prod * (1.0 - tanh * tanh)
+                grad_ref[rows, cols] = grad.astype(BF16)
+                terms = prod * tanh - ratio * grad
+                total = total + jnp.sum(terms.reshape(piece // 8, 8, 256), axis=0)
+            csum_ref[:, cols] = total
+        if start:
+            products(start - chunk)
+    products(width - chunk)
 
 
 def reduce_kernel(
@@ -253,7 +283,7 @@
             jax.ShapeDtypeStruct((rows, width), F32),
             jax.ShapeDtypeStruct((rows, width), F32),
         ),
-        in_specs=[vmem] * 4,
+        in_specs=[pl.BlockSpec(memory_space=pl.ANY)] * 4,
         out_specs=(vmem,) * 4,
         scratch_shapes=[
             pltpu.VMEM(folded, BF16),
@@ -261,19 +291,23 @@
             pltpu.VMEM(folded, BF16),
             pltpu.VMEM((dn,) + folded, BF16),
             pltpu.VMEM((tn, group, hidden), BF16),
+            pltpu.VMEM((rows, width), BF16),
+            pltpu.VMEM((1, width), F32),
+            pltpu.VMEM((LANES, LANES), F32),
             sems(tn - 1), sems(tn - 1), sems(dn - 1),
+            pltpu.SemaphoreType.DMA((4,)),
         ],
         compiler_params=pltpu.CompilerParams(
-            collective_id=0, has_side_effects=True, vmem_limit_bytes=48 * 2**20
+            collective_id=0, has_side_effects=True, vmem_limit_bytes=62 * 2**20
         ),
         name="gather",
     )(tokens, clip_act.reshape(1, -1), cotangent, had)
 
     depth = 256
-    chunk = next(c for c in (1024, 768, 512, 256, 128) if hidden % c == 0)
+    chunk = next(c for c in (512, 256) if hidden % c == 0)
     clip_row = clip_weight.reshape(1, -1)
     grad, act_prod, proj, clip_sum = pl.pallas_call(
-        functools.partial(weight_kernel, chunk),
+        functools.partial(weight_kernel, chunk, 64),
         grid=(width // depth,),
         out_shape=(
             jax.ShapeDtypeStruct((width, hidden), BF16),
@@ -284,7 +318,6 @@
         in_specs=[
             pl.BlockSpec((all_rows, depth), lambda i: (0, i)),
             pl.BlockSpec((all_rows, hidden), lambda i: (0, 0)),
-            pl.BlockSpec((1, hidden), lambda i: (0, 0)),
             pl.BlockSpec((1, hidden), lambda i: (0, 0)),
             pl.BlockSpec((depth, hidden), lambda i: (i, 0)),
         ],
@@ -294,9 +327,10 @@
             pl.BlockSpec((all_rows, hidden), lambda i: (0, 0)),
             pl.BlockSpec((8, hidden), lambda i: (0, 0)),
         ),
+        scratch_shapes=[pltpu.VMEM((depth, hidden), BF16), pltpu.VMEM((1, hidden), F32)],
         compiler_params=pltpu.CompilerParams(vmem_limit_bytes=48 * 2**20),
         name="weights",
-    )(all_act, all_cot, clip_row, 1.0 / clip_row, weight)
+    )(all_act, all_cot, clip_row, weight)
 
     projected, token_grad, clip_act_grad, clip_weight_grad = pl.pallas_call(
         functools.partial(reduce_kernel, tn, dn, norm),

time: 122 us -> 108 us (0.89)
  Pallas kernels: 114 us -> 102 us
    pallas_call x1, Pallas kernels: 66.7 us -> 52.6 us  [body(): pl.pallas_call(functools.partial(weight_kernel, chunk, 64), grid=(width /...]
    pallas_call x1, Pallas kernels: 20.2 us -> 22.2 us  [body(): pl.pallas_call(functools.partial(gather_kernel, tn, dn, norm), out_shape=...]
where the time goes in v2:
time: 108 us
  Pallas kernels  102 us (94%)
  local copies, waits for them, and re-layouts  5.44 us (5%)
    pallas_call x1, Pallas kernels, body(): pl.pallas_call(functools.partial(weight_kernel, chunk, 64), grid=(width /...  52.6 us
    pallas_call x1, Pallas kernels, body(): pl.pallas_call(functools.partial(reduce_kernel, tn, dn, norm), out_shape=...  27.2 us
    pallas_call x1, Pallas kernels, body(): pl.pallas_call(functools.partial(gather_kernel, tn, dn, norm), out_shape=...  22.2 us
    unnamed x16, local copies, waits for them, and re-layouts  5.44 us

profile of v2, /device:TPU:0, one launch (start us, length us, event | category | flops | bytes accessed | tf_op | source)
XLA Modules:
  0.0 108.1 jit_solution(1035996241349289909)
XLA Ops:
  0.6 0.0 copy-start.2
  0.6 22.2 %gather.1 = (bf16[64,6144]{1,0:T(8,128)(2,1)}, bf16[64,4096]{1,0:T(8,128)(2,1)}, f32[8,4096]{1,0:T(8,128)}, f32[8,4096]{1,0:T(8,128)}) custom-call(bf16[8,4096]{1,0:T(8,128)(2,1)} %tok_ref.1, f32[1,4096]{1,0:T(1,128)} %bitcast.7, bf16[16,6144]{1,0:T(8,128)(2,1)} %cot_ref.1, f32[128,128]{1,0:T(8,128)} %constant.2.clone.had_ref), custom_call_target="tpu_custom_call" | custom-call | tf_op jit(solution)/shard_map/gather/pallas_call | solution.py:278
  22.8 0.0 copy-start
  22.8 1.1 %copy-done = bf16[64,6144]{1,0:T(8,128)(2,1)S(1)} copy-done((bf16[64,6144]{1,0:T(8,128)(2,1)S(1)}, bf16[64,6144]{1,0:T(8,128)(2,1)}, u32[]{:S(2)}) %copy-start) | copy-done | bytes 786456
  24.0 0.0 copy-start.1
  24.0 1.0 copy-done.1
  25.0 0.0 copy-start.5
  25.0 0.7 copy-done.5
  25.7 0.0 copy-start.3
  25.7 0.0 copy-start.4
  25.7 52.6 %weights.1 = (bf16[4096,6144]{1,0:T(8,128)(2,1)}, f32[64,4096]{1,0:T(8,128)S(1)}, f32[64,6144]{1,0:T(8,128)S(1)}, f32[8,6144]{1,0:T(8,128)S(1)}) custom-call(bf16[64,4096]{1,0:T(8,128)(2,1)S(1)} %copy-done.1, bf16[64,6144]{1,0:T(8,128)(2,1)S(1)} %copy-done, f32[1,6144]{1,0:T(1,128)S(1)} %bitcast.4, bf16[4096,6144]{1,0:T(8,128)(2,1)} %w_ref.1), custom_call_target="tpu_custom_call" | custom-call | tf_op jit(solution)/shard_map/weights/pallas_call | solution.py:309
  78.4 0.0 copy-done.2
  78.4 0.0 copy-done.3
  78.4 0.0 copy-done.4
  78.4 27.2 %reduce.1 = (bf16[16,6144]{1,0:T(8,128)(2,1)S(1)}, bf16[8,4096]{1,0:T(8,128)(2,1)S(1)}, f32[1,4096]{1,0:T(1,128)S(1)}, f32[1,6144]{1,0:T(1,128)S(1)}) custom-call(f32[64,4096]{1,0:T(8,128)S(1)} %get-tuple-element.19.actp_ref, f32[64,6144]{1,0:T(8,128)S(1)} %get-tuple-element.20.proj_ref, f32[8,6144]{1,0:T(8,128)S(1)} %get-tuple-element.21.csum_ref, ...), custom_call_target="tpu_custom_call" | custom-call | tf_op jit(solution)/shard_map/reduce/pallas_call | solution.py:335
  105.6 0.7 copy.15
  106.2 0.6 copy.16
  106.9 0.6 copy.17
  107.5 0.6 copy.18
Async XLA Ops:
  0.6 77.7 %copy-start.2 = (f32[128,128]{1,0:T(8,128)S(1)}, f32[128,128]{1,0:T(8,128)}, u32[]{:S(2)}) copy-start(f32[128,128]{1,0:T(8,128)} %constant.2.clone.had_ref) | copy-start | bytes 196612
  22.8 1.1 %copy-start = (bf16[64,6144]{1,0:T(8,128)(2,1)S(1)}, bf16[64,6144]{1,0:T(8,128)(2,1)}, u32[]{:S(2)}) copy-start(bf16[64,6144]{1,0:T(8,128)(2,1)} %get-tuple-element.18.cot_ref) | copy-start | bytes 2359300
  24.0 1.0 copy-start.1
  25.0 0.7 copy-start.5
  25.7 52.6 %copy-start.3 = (f32[8,4096]{1,0:T(8,128)S(1)}, f32[8,4096]{1,0:T(8,128)}, u32[]{:S(2)}) copy-start(f32[8,4096]{1,0:T(8,128)} %get-tuple-element.22.slope_ref) | copy-start | bytes 393220
  25.7 52.6 %copy-start.4 = (f32[8,4096]{1,0:T(8,128)S(1)}, f32[8,4096]{1,0:T(8,128)}, u32[]{:S(2)}) copy-start(f32[8,4096]{1,0:T(8,128)} %get-tuple-element.23.edge_ref) | copy-start | bytes 393220
